TPU v7x, 32 devices: a whole 2x2x4 slice. The times are simulated.
32 devices in a mesh: pole: 2 (over y), prow: 4 (over z), pcol: 4 (over x, core).
Axes of the slice: x: 2, y: 2, z: 4, core: 2. Of those that a mesh axis runs over, the one named last changes fastest.
Arguments:
- ainv: bfloat16 [4, 1024, 1024], P('pole', 'prow', 'pcol'), parts along dimension 0, may hold values from -0.1875 to 0.1875
- panel: bfloat16 [4, 4, 4, 64, 256], P('pole', 'pcol', 'prow'), parts along dimension 0, may hold values from -6 to 6
- upanel: bfloat16 [4, 256, 1024], P('pole', None, 'prow'), parts along dimension 0, may hold values from -0.1875 to 0.1875
- dinv: float32 [4, 256, 256], P('pole'), parts along dimension 0, may hold values from -6 to 6
- pattern: int32 [8, 8], P('prow', 'pcol'), may hold values from 0 to 1, as said below
Outputs:
- column: bfloat16 [4, 1024, 256], P('pole', 'prow'), parts along dimension 0
- diagonal: float32 [4, 256, 256], P('pole'), parts along dimension 0
There are 2 independent parts, one for each index of `pole`. A program takes and returns all parts, laid end to end along the dimension named above; an argument that names none is the same for every part. Nothing has to cross between parts.
Inputs may be any that keep to these rules, and one draw needn't show every extreme that they name: pattern[i, i] = 1 for every block i; the number of present blocks varies from row to row.
All inputs are finite; a program needn't handle non-finite values.
Results may differ from a plain program's by a relative error of at most 0.0004.
Values may be sent and summed in bfloat16 or wider, within the bound.
A program may use at most 64 MiB of HBM per device.

v0:
```python
import jax
import jax.numpy as jnp
from jax import lax
from jax.sharding import PartitionSpec as P

BLK = 128


def complex_dot(left_re, left_im, right_re, right_im):
    real = jnp.dot(left_re, right_re, preferred_element_type=jnp.float32) - jnp.dot(
        left_im, right_im, preferred_element_type=jnp.float32
    )
    imag = jnp.dot(left_re, right_im, preferred_element_type=jnp.float32) + jnp.dot(
        left_im, right_re, preferred_element_type=jnp.float32
    )
    return (real, imag)


def upper_terms(up_full, column_full):
    hi = lax.Precision.HIGHEST
    d_re = jnp.dot(up_full[0], column_full[0], precision=hi) - jnp.dot(
        up_full[1], column_full[1], precision=hi
    )
    d_im = jnp.dot(up_full[0], column_full[1], precision=hi) + jnp.dot(
        up_full[1], column_full[0], precision=hi
    )
    return jnp.stack([d_re, d_im])


def per_device(ainv, panel, upanel, dinv, pattern):
    local_cols = ainv.shape[2]
    row_blocks = pattern.shape[0]
    col_blocks = pattern.shape[1]
    width = panel.shape[4]
    weights = pattern.astype(jnp.bfloat16)
    masked = (
        ainv.reshape(2, row_blocks, BLK, col_blocks, BLK) * weights[None, :, None, :, None]
    ).reshape(ainv.shape)
    gathered = lax.all_gather(panel, "prow", axis=2, tiled=True).reshape(2, local_cols, width)
    real, imag = complex_dot(masked[0], masked[1], gathered[0], gathered[1])
    partial_value = jnp.stack([-real, -imag])
    column_full = lax.psum(partial_value, "pcol")
    column = column_full.astype(jnp.bfloat16)
    up_full = upanel.astype(jnp.float32)
    total = lax.psum(upper_terms(up_full, column_full), "prow")
    diagonal = dinv - total
    return (column, diagonal)


def solution(mesh):
    in_specs = (
        P("pole", "prow", "pcol"),
        P("pole", "pcol", "prow", None, None),
        P("pole", None, "prow"),
        P("pole", None, None),
        P("prow", "pcol"),
    )
    out_specs = (P("pole", "prow", None), P("pole", None, None))
    return jax.shard_map(
        per_device, mesh=mesh, in_specs=in_specs, out_specs=out_specs, check_vma=False
    )
```

profile of v0, /device:TPU:0, one launch (start us, length us, event | category | flops | bytes accessed | tf_op | source)
XLA Modules:
  0.0 113.0 jit_solution(8567726692748681059)
XLA Ops:
  7.2 0.7 convert_element_type.7
  7.9 1.0 reshape.18
  8.9 0.3 broadcast_multiply_fusion
  9.2 0.2 fusion.26
  9.4 0.6 copy-done.3
  10.1 15.6 %all_gather.3 = bf16[2,1,4,64,256]{4,3,2,1,0:T(8,128)(2,1)S(1)} all-gather(bf16[2,1,1,64,256]{4,3,2,1,0:T(8,128)(2,1)S(1)} %copy-done.3), channel_id=1, replica_groups=mesh['pole'=2,'prow'=4,'pcol'=4] {'prow'}, dimensions={2}, use_global_device_ids=true | all-gather | bytes 327680 | tf_op jit(solution)/shard_map/all_gather | solution.py:39
  25.7 0.2 fusion.10
  25.9 0.2 fusion.12
  26.1 0.2 fusion.3
  26.3 0.2 fusion.5
  26.5 0.8 pad_maximum_fusion
  27.3 0.0 all-reduce.5.cloned.1.call-start
  27.4 34.8 %all-reduce.3.cloned.1.call-done = f32[2,256,256]{2,1,0:T(8,128)} async-done(((f32[2,256,256]{2,1,0:T(8,128)}), f32[2,256,256]{2,1,0:T(8,128)}) %all-reduce.3.cloned.1.call-update) | async-done | bytes 524304 | tf_op jit(solution)/shard_map/psum | solution.py:42
  62.2 1.4 %fusion.7 = f32[256,256]{1,0:T(8,128)S(1)} fusion(f32[2,256,256]{2,1,0:T(8,128)} %all-reduce.3.cloned.1.call-done, bf16[2,256,256]{2,1,0:T(8,128)(2,1)S(1)} %copy-done.1), kind=kOutput, calls=%fused_computation.15 | convolution fusion | flops 201326592 | bytes 655360 | tf_op jit(solution)/shard_map/dot_general | solution.py:24
  63.6 0.4 fusion.6
  64.0 0.4 fusion
  64.4 0.4 fusion.1
  64.8 0.8 pad_maximum_fusion.1
  65.6 1.0 copy-done.2
  66.7 0.2 copy.7
  66.9 0.7 convert_element_type.8
  67.6 36.5 %all-reduce.5.cloned.1.call-done = f32[2,256,256]{1,2,0:T(8,128)} async-done(((f32[2,256,256]{1,2,0:T(8,128)}), f32[2,256,256]{1,2,0:T(8,128)}) %all-reduce.5.cloned.1.call-update) | async-done | bytes 524304 | tf_op jit(solution)/shard_map/psum | solution.py:45
  104.1 1.1 sub.15
  105.2 1.0 copy.8
  (10 shorter events, 0.1 us)
Async XLA Ops:
  7.2 55.0 %all-reduce.3.cloned.1.call-start = ((), (), s32[]{:S(2)}) async-start(), calls=%async_computation | async-start | bytes 1048576 | tf_op jit(solution)/shard_map/psum | solution.py:42
  9.2 0.8 copy-start.3
  27.3 34.9 %copy-start.1 = (bf16[2,256,256]{2,1,0:T(8,128)(2,1)S(1)}, bf16[2,256,256]{2,1,0:T(8,128)(2,1)}, u32[]{:S(2)}) copy-start(bf16[2,256,256]{2,1,0:T(8,128)(2,1)} %param.7) | copy-start | bytes 786436
  27.3 76.8 %all-reduce.5.cloned.1.call-start = ((), (), s32[]{:S(2)}) async-start(), calls=%async_computation.1 | async-start | bytes 1048576 | tf_op jit(solution)/shard_map/psum | solution.py:45
  62.2 1.4 %copy-start = (f32[2,256,256]{2,1,0:T(8,128)S(1)}, f32[2,256,256]{2,1,0:T(8,128)}, u32[]{:S(2)}) copy-start(f32[2,256,256]{2,1,0:T(8,128)} %all-reduce.3.cloned.1.call-done) | copy-start | bytes 1572868
  65.6 1.0 copy-start.2
Sparse Core Ops, SparseCore 0:
  27.4 34.6 all-reduce.2
  65.8 38.2 all-reduce.4
where the time goes:
time: 113 us
  waiting for transfers between devices  71.3 us (63%)
  blocking collectives  15.6 us (14%)
  between operations  14.1 us (12%)
  other arithmetic  4.48 us (4%)
  local copies, waits for them, and re-layouts  4.07 us (4%)
  matrix products  3.3 us (3%)
    psum x1, waiting for transfers between devices, per_device(): total = lax.psum(upper_terms(up_full, column_full), 'prow')  36.5 us
    psum x1, waiting for transfers between devices, per_device(): column_full = lax.psum(partial_value, 'pcol')  34.8 us
    all_gather x1, blocking collectives, per_device(): lax.all_gather(panel, 'prow', axis=2, tiled=True)  15.6 us
    unnamed x10, local copies, waits for them, and re-layouts  2.86 us
  transfers between devices with their start and end apart: 2, of which 2 were waited for; matrix products, arithmetic and copies ran while one was open for 1% of the time, Pallas kernels for 0%

commit v1 on v0

v1 whole, which is shorter than its diff:
```python
import functools

import jax
import jax.numpy as jnp
from jax import lax
from jax.experimental import pallas as pl
from jax.experimental.pallas import tpu as pltpu
from jax.sharding import PartitionSpec as P

BLK = 128
MESH = pl.DeviceIdType.MESH
F32 = jnp.float32
BF16 = jnp.bfloat16


def kernel(n, ainv, panel, upanel, dinv, pattern, col_out, diag_out,
           a_v, u_v, d_v, low, m_v, um_v, part, core_in, cx, tbuf, x_in, xc_in,
           sbuf, z_in, dall, call,
           loc_sem, p_send, p_recv, b_send, b_recv, x_send, x_recv, z_send, z_recv,
           gz_send, gz_recv, gx_send, gx_recv, gc_send, gc_recv, c_send, c_recv):
    pole = lax.axis_index("pole")
    me = lax.axis_index("prow")
    j = lax.axis_index("pcol")
    h = lax.rem(j, 2)
    x = j // 2
    rows = panel.shape[3]
    z_peer = [lax.rem(me + d, n) for d in range(n)]
    z_from = [lax.rem(me + n - d, n) for d in range(n)]
    sib = (pole, me, j + 1 - 2 * h)
    xp = (pole, me, lax.rem(j + 2, 4))

    def remote(src, dst, send, recv, device):
        return pltpu.make_async_remote_copy(
            src_ref=src, dst_ref=dst, send_sem=send, recv_sem=recv,
            device_id=device, device_id_type=MESH)

    my_rows = pl.ds(pl.multiple_of(me * rows, rows), rows)
    locs = [
        pltpu.make_async_copy(panel.at[:, 0, 0], low.at[:, my_rows], loc_sem.at[0]),
        pltpu.make_async_copy(ainv, a_v, loc_sem.at[1]),
        pltpu.make_async_copy(upanel, u_v, loc_sem.at[2]),
        pltpu.make_async_copy(dinv, d_v, loc_sem.at[3]),
    ]
    for c in locs:
        c.start()
    barrier = pltpu.get_barrier_semaphore()
    others = [(pole, z_peer[d], j) for d in range(1, n)] + [sib, xp]
    for dev in others:
        pl.semaphore_signal(barrier, inc=1, device_id=dev, device_id_type=MESH)
    pl.semaphore_wait(barrier, len(others))

    sends = []
    gathers = []
    for d in range(1, n):
        c = remote(panel.at[:, 0, 0], low.at[:, my_rows], p_send.at[d], p_recv.at[d],
                   (pole, z_peer[d], j))
        c.start()
        gathers.append(c)
        sends.append(c)

    locs[1].wait()
    w = a_v.shape[2]
    for bi in range(pattern.shape[0]):
        for bj in range(pattern.shape[1]):
            wt = pattern[bi, bj].astype(F32)
            rs = slice(bi * BLK, (bi + 1) * BLK)
            cs = slice(bj * BLK, (bj + 1) * BLK)
            r0, c0 = bi * BLK, bj * BLK
            re = a_v[0, rs, cs].astype(F32) * wt
            im = a_v[1, rs, cs].astype(F32) * wt
            nre = (-re).astype(BF16)
            m_v[r0:r0 + BLK, c0:c0 + BLK] = nre
            m_v[w + r0:w + r0 + BLK, w + c0:w + c0 + BLK] = nre
            m_v[r0:r0 + BLK, w + c0:w + c0 + BLK] = im.astype(BF16)
            m_v[w + r0:w + r0 + BLK, c0:c0 + BLK] = (-im).astype(BF16)
    locs[2].wait()
    um_v[:w, :w] = u_v[0]
    um_v[w:, w:] = u_v[0]
    um_v[:w, w:] = -u_v[1]
    um_v[w:, :w] = u_v[1]
    locs[0].wait()
    for c in gathers:
        c.wait_recv()

    prod = jnp.dot(m_v[...], low[...].reshape(2 * w, w), preferred_element_type=F32)
    part[0] = prod[:, :BLK]
    part[1] = prod[:, BLK:]
    c = remote(part.at[1 - h], core_in, b_send, b_recv, sib)
    c.start()
    c.wait_recv()
    sends.append(c)

    half = part[h] + core_in[...]
    cx[...] = half.reshape(cx.shape)
    hi = half.astype(BF16)
    lo = (half - hi.astype(F32)).astype(BF16)
    t = jnp.dot(um_v[...], jnp.concatenate([hi, lo], axis=1), preferred_element_type=F32)
    tbuf[...] = (t[:, :BLK] + t[:, BLK:]).reshape(tbuf.shape)
    dx = remote(tbuf.at[:, 1 - x], x_in, x_send.at[0], x_recv.at[0], xp)
    dx.start()
    cxc = remote(cx.at[:, 1 - x], xc_in, x_send.at[1], x_recv.at[1], xp)
    cxc.start()
    sends += [dx, cxc]
    dx.wait_recv()
    sbuf[...] = tbuf[:, x] + x_in[...]
    zs = []
    for d in range(1, n):
        c = remote(sbuf.at[:, z_peer[d]], z_in.at[d], z_send.at[d], z_recv.at[d],
                   (pole, z_peer[d], j))
        c.start()
        zs.append(c)
    sends += zs

    cxc.wait_recv()
    call[h, x] = (cx[:, x] + xc_in[...]).astype(BF16)
    col_x = remote(call.at[h, x], call.at[h, x], c_send.at[0], c_recv.at[0], xp)
    col_s = remote(call.at[h, x], call.at[h, x], c_send.at[1], c_recv.at[1], sib)
    col_x.start()
    col_s.start()
    sends += [col_x, col_s]

    total = sbuf[:, me]
    for d in range(1, n):
        zs[d - 1].wait_recv()
        total = total + z_in[d]
    dall[h, x, me] = total

    def piece(side, d, dev, send, recv):
        slot = dall.at[h, side, z_from[d]]
        c = remote(slot, slot, send, recv, dev)
        c.start()
        sends.append(c)
        return c

    mine = dall.at[h, x, me]
    gz = []
    for d in range(1, n):
        c = remote(mine, mine, gz_send.at[d], gz_recv.at[d], (pole, z_peer[d], j))
        c.start()
        sends.append(c)
        gz.append(c)
    gx = [piece(x, 0, xp, gx_send.at[0], gx_recv.at[0])]
    gc = [piece(x, 0, sib, gc_send.at[0], gc_recv.at[0])]

    col_x.wait_recv()
    other = call.at[h, 1 - x]
    col_f = remote(other, other, c_send.at[2], c_recv.at[2], sib)
    col_f.start()
    sends.append(col_f)

    for d in range(1, n):
        gz[d - 1].wait_recv()
        gx.append(piece(x, d, xp, gx_send.at[d], gx_recv.at[d]))
        gc.append(piece(x, d, sib, gc_send.at[d], gc_recv.at[d]))
    for d in range(n):
        gx[d].wait_recv()
        gc.append(piece(1 - x, d, sib, gc_send.at[n + d], gc_recv.at[n + d]))

    col_s.wait_recv()
    col_f.wait_recv()
    for a in range(2):
        for b in range(2):
            col_out[:, b * BLK:(b + 1) * BLK, a * BLK:(a + 1) * BLK] = call[a, b]
    locs[3].wait()
    for c in gc:
        c.wait_recv()
    pr = dall.shape[4]
    for a in range(2):
        for b in range(2):
            for k in range(n):
                rs = slice(b * BLK + k * pr, b * BLK + (k + 1) * pr)
                cs = slice(a * BLK, (a + 1) * BLK)
                diag_out[:, rs, cs] = d_v[:, rs, cs] - dall[a, b, k]
    for c in sends:
        c.wait_send()


def fused(n, ainv, panel, upanel, dinv, pattern):
    w = ainv.shape[2]
    pr = BLK // n
    dma = pltpu.SemaphoreType.DMA
    hbm = pl.BlockSpec(memory_space=pl.ANY)
    vmem = pl.BlockSpec(memory_space=pltpu.VMEM)
    return pl.pallas_call(
        functools.partial(kernel, n),
        out_shape=(
            jax.ShapeDtypeStruct((2, w, w), BF16),
            jax.ShapeDtypeStruct((2, w, w), F32),
        ),
        in_specs=[hbm, hbm, hbm, hbm, pl.BlockSpec(memory_space=pltpu.SMEM)],
        out_specs=(vmem, vmem),
        scratch_shapes=[
            pltpu.VMEM((2, w, w), BF16),
            pltpu.VMEM((2, w, w), BF16),
            pltpu.VMEM((2, w, w), F32),
            pltpu.VMEM((2, w, w), BF16),
            pltpu.VMEM((2 * w, 2 * w), BF16),
            pltpu.VMEM((2 * w, 2 * w), BF16),
            pltpu.VMEM((2, 2 * w, BLK), F32),
            pltpu.VMEM((2 * w, BLK), F32),
            pltpu.VMEM((2, 2, BLK, BLK), F32),
            pltpu.VMEM((2, 2, n, pr, BLK), F32),
            pltpu.VMEM((2, n, pr, BLK), F32),
            pltpu.VMEM((2, BLK, BLK), F32),
            pltpu.VMEM((2, n, pr, BLK), F32),
            pltpu.VMEM((n, 2, pr, BLK), F32),
            pltpu.VMEM((2, 2, n, 2, pr, BLK), F32),
            pltpu.VMEM((2, 2, 2, BLK, BLK), BF16),
            dma((4,)),
            dma((n,)), dma((n,)),
            dma, dma,
            dma((2,)), dma((2,)),
            dma((n,)), dma((n,)),
            dma((n,)), dma((n,)),
            dma((n,)), dma((n,)),
            dma((2 * n,)), dma((2 * n,)),
            dma((3,)), dma((3,)),
        ],
        compiler_params=pltpu.CompilerParams(
            collective_id=0, has_side_effects=True, vmem_limit_bytes=48 * 2**20),
        cost_estimate=pl.CostEstimate(
            flops=12 * w**3, bytes_accessed=12 * w * w, transcendentals=0),
    )(ainv, panel, upanel, dinv, pattern)


def complex_dot(left_re, left_im, right_re, right_im):
    real = jnp.dot(left_re, right_re, preferred_element_type=F32) - jnp.dot(
        left_im, right_im, preferred_element_type=F32
    )
    imag = jnp.dot(left_re, right_im, preferred_element_type=F32) + jnp.dot(
        left_im, right_re, preferred_element_type=F32
    )
    return (real, imag)


def upper_terms(up_full, column_full):
    hi = lax.Precision.HIGHEST
    d_re = jnp.dot(up_full[0], column_full[0], precision=hi) - jnp.dot(
        up_full[1], column_full[1], precision=hi
    )
    d_im = jnp.dot(up_full[0], column_full[1], precision=hi) + jnp.dot(
        up_full[1], column_full[0], precision=hi
    )
    return jnp.stack([d_re, d_im])


def general(ainv, panel, upanel, dinv, pattern):
    local_cols = ainv.shape[2]
    row_blocks = pattern.shape[0]
    col_blocks = pattern.shape[1]
    width = panel.shape[4]
    weights = pattern.astype(BF16)
    masked = (
        ainv.reshape(2, row_blocks, BLK, col_blocks, BLK) * weights[None, :, None, :, None]
    ).reshape(ainv.shape)
    gathered = lax.all_gather(panel, "prow", axis=2, tiled=True).reshape(2, local_cols, width)
    real, imag = complex_dot(masked[0], masked[1], gathered[0], gathered[1])
    column_full = lax.psum(jnp.stack([-real, -imag]), "pcol")
    column = column_full.astype(BF16)
    total = lax.psum(upper_terms(upanel.astype(F32), column_full), "prow")
    return (column, dinv - total)


def solution(mesh):
    n = mesh.shape["prow"]

    def per_device(ainv, panel, upanel, dinv, pattern):
        square = ainv.shape[1:] == (2 * BLK, 2 * BLK) and panel.shape[4] == 2 * BLK
        if n == 4 and mesh.shape["pcol"] == 4 and square:
            return fused(n, ainv, panel, upanel, dinv, pattern)
        return general(ainv, panel, upanel, dinv, pattern)

    in_specs = (
        P("pole", "prow", "pcol"),
        P("pole", "pcol", "prow", None, None),
        P("pole", None, "prow"),
        P("pole", None, None),
        P("prow", "pcol"),
    )
    out_specs = (P("pole", "prow", None), P("pole", None, None))
    return jax.shard_map(
        per_device, mesh=mesh, in_specs=in_specs, out_specs=out_specs, check_vma=False
    )
```

time: 113 us -> 38.7 us (0.34)
  waiting for transfers between devices: 71.3 us -> 0 us
  Pallas kernels: 0 us -> 31.6 us
  blocking collectives: 15.6 us -> 0 us
  between operations: 14.1 us -> 0.65 us
  other arithmetic: 4.48 us -> 0 us
  matrix products: 3.3 us -> 0 us
  local copies, waits for them, and re-layouts: 4.07 us -> 5.95 us
    psum x2 -> x0, waiting for transfers between devices: 71.3 us -> none  [the longest x1 36.5 us: per_device(): total = lax.psum(upper_terms(up_full, column_full), 'prow')]
    pallas_call x0 -> x1, Pallas kernels: none -> 31.6 us  [fused(): pl.pallas_call(functools.partial(kernel, n), out_shape=(jax.ShapeDtypeStr...]
    all_gather x1 -> x0, blocking collectives: 15.6 us -> none  [per_device(): lax.all_gather(panel, 'prow', axis=2, tiled=True)]
    dot_general x8 -> x0, matrix products: 3.3 us -> none  [the longest x1 1.4 us: upper_terms(): jnp.dot(up_full[0], column_full[1], precision=hi)]
    unnamed x10 -> x12, local copies, waits for them, and re-layouts: 2.86 us -> 5.95 us
    another operation x2 -> x0, other arithmetic: 1.66 us -> none  [the longest x1 0.83 us: per_device(): partial_value = jnp.stack([-real, -imag])]
    convert_element_type x2 -> x0, other arithmetic: 1.41 us -> none  [the longest x1 0.73 us: per_device(): column = column_full.astype(jnp.bfloat16)]
  transfers between devices with their start and end apart: 2 -> 0, of which waited for: 2 -> 0; matrix products, arithmetic and copies ran while one was open for 1% -> 0% of each run, Pallas kernels for 0% -> 0%
where the time goes in v1:
time: 38.7 us; the launch traced here: 38.2 us
  Pallas kernels  31.6 us (82%)
  local copies, waits for them, and re-layouts  5.95 us (15%)
  between operations  0.65 us (2%)
    pallas_call x1, Pallas kernels, fused(): pl.pallas_call(functools.partial(kernel, n), out_shape=(jax.ShapeDtypeStr...  31.6 us
    unnamed x12, local copies, waits for them, and re-layouts  5.95 us

profile of v1, /device:TPU:0, one launch (start us, length us, event | category | flops | bytes accessed | tf_op | source)
XLA Modules:
  0.0 38.2 jit_solution(6461199576197438004)
XLA Ops:
  0.6 0.0 copy-start
  0.6 1.0 %copy-done = f32[2,256,256]{2,1,0:T(8,128)S(1)} copy-done((f32[2,256,256]{2,1,0:T(8,128)S(1)}, f32[2,256,256]{2,1,0:T(8,128)}, u32[]{:S(2)}) %copy-start) | copy-done | bytes 524312
  1.7 0.0 copy-start.1
  1.7 0.9 %copy-done.1 = bf16[2,256,256]{2,1,0:T(8,128)(2,1)S(1)} copy-done((bf16[2,256,256]{2,1,0:T(8,128)(2,1)S(1)}, bf16[2,256,256]{2,1,0:T(8,128)(2,1)}, u32[]{:S(2)}) %copy-start.1) | copy-done | bytes 262168
  2.6 0.0 copy-start.2
  2.6 0.9 %copy-done.2 = bf16[2,256,256]{2,1,0:T(8,128)(2,1)S(1)} copy-done((bf16[2,256,256]{2,1,0:T(8,128)(2,1)S(1)}, bf16[2,256,256]{2,1,0:T(8,128)(2,1)}, u32[]{:S(2)}) %copy-start.2) | copy-done | bytes 262168
  3.6 0.0 copy-start.3
  3.6 0.8 %copy-done.3 = bf16[2,1,1,64,256]{4,3,2,1,0:T(8,128)(2,1)S(1)} copy-done((bf16[2,1,1,64,256]{4,3,2,1,0:T(8,128)(2,1)S(1)}, bf16[2,1,1,64,256]{4,3,2,1,0:T(8,128)(2,1)}, u32[]{:S(2)}) %copy-start.3) | copy-done | bytes 65560
  4.4 0.0 copy-start.4
  4.4 0.7 %copy-done.4 = s32[2,2]{1,0:T(2,128)S(1)} copy-done((s32[2,2]{1,0:T(2,128)S(1)}, s32[2,2]{1,0:T(2,128)}, u32[]{:S(2)}) %copy-start.4) | copy-done | bytes 40
  5.1 31.6 %shard_map.68 = (bf16[2,256,256]{2,1,0:T(8,128)(2,1)S(1)}, f32[2,256,256]{2,1,0:T(8,128)S(1)}) custom-call(bf16[2,256,256]{2,1,0:T(8,128)(2,1)S(1)} %copy-done.1, bf16[2,1,1,64,256]{4,3,2,1,0:T(8,128)(2,1)S(1)} %copy-done.3, bf16[2,256,256]{2,1,0:T(8,128)(2,1)S(1)} %copy-done.2, f32[2,256,256]{2,1,0:T(8,128)S(1)} %copy-done, s32[2,2]{1,0:T(2,128)S(1)} %copy-done.4), custom_call_target="tpu_custom_call" | custom-call | flops 201326592 | bytes 786432 | tf_op jit(solution)/shard_map/pallas_call | solution.py:184
  36.8 0.7 %copy.9 = bf16[2,256,256]{2,1,0:T(8,128)(2,1)} copy(bf16[2,256,256]{2,1,0:T(8,128)(2,1)S(1)} %get-tuple-element.4) | data formatting | bytes 524288
  37.5 0.8 %copy.10 = f32[2,256,256]{2,1,0:T(8,128)} copy(f32[2,256,256]{2,1,0:T(8,128)S(1)} %get-tuple-element.5) | data formatting | bytes 1048576
Async XLA Ops:
  0.6 1.0 %copy-start = (f32[2,256,256]{2,1,0:T(8,128)S(1)}, f32[2,256,256]{2,1,0:T(8,128)}, u32[]{:S(2)}) copy-start(f32[2,256,256]{2,1,0:T(8,128)} %dinv.1) | copy-start | bytes 1572868
  1.7 0.9 %copy-start.1 = (bf16[2,256,256]{2,1,0:T(8,128)(2,1)S(1)}, bf16[2,256,256]{2,1,0:T(8,128)(2,1)}, u32[]{:S(2)}) copy-start(bf16[2,256,256]{2,1,0:T(8,128)(2,1)} %ainv.1) | copy-start | bytes 786436
  2.6 0.9 %copy-start.2 = (bf16[2,256,256]{2,1,0:T(8,128)(2,1)S(1)}, bf16[2,256,256]{2,1,0:T(8,128)(2,1)}, u32[]{:S(2)}) copy-start(bf16[2,256,256]{2,1,0:T(8,128)(2,1)} %upanel.1) | copy-start | bytes 786436
  3.6 0.8 %copy-start.3 = (bf16[2,1,1,64,256]{4,3,2,1,0:T(8,128)(2,1)S(1)}, bf16[2,1,1,64,256]{4,3,2,1,0:T(8,128)(2,1)}, u32[]{:S(2)}) copy-start(bf16[2,1,1,64,256]{4,3,2,1,0:T(8,128)(2,1)} %panel.1) | copy-start | bytes 196612
  4.4 0.7 %copy-start.4 = (s32[2,2]{1,0:T(2,128)S(1)}, s32[2,2]{1,0:T(2,128)}, u32[]{:S(2)}) copy-start(s32[2,2]{1,0:T(2,128)} %pattern.1) | copy-start | bytes 52

commit v2 on v1

--- a/solution.py
+++ b/solution.py
@@ -14,7 +14,7 @@
 
 
 def kernel(n, ainv, panel, upanel, dinv, pattern, col_out, diag_out,
-           a_v, u_v, d_v, low, m_v, um_v, part, core_in, cx, tbuf, x_in, xc_in,
+           pat_s, a_v, u_v, d_v, low, m_v, um_v, part, core_in, cx, tbuf, x_in, xc_in,
            sbuf, z_in, dall, call,
            loc_sem, p_send, p_recv, b_send, b_recv, x_send, x_recv, z_send, z_recv,
            gz_send, gz_recv, gx_send, gx_recv, gc_send, gc_recv, c_send, c_recv):
@@ -40,6 +40,7 @@
         pltpu.make_async_copy(ainv, a_v, loc_sem.at[1]),
         pltpu.make_async_copy(upanel, u_v, loc_sem.at[2]),
         pltpu.make_async_copy(dinv, d_v, loc_sem.at[3]),
+        pltpu.make_async_copy(pattern, pat_s, loc_sem.at[4]),
     ]
     for c in locs:
         c.start()
@@ -59,10 +60,11 @@
         sends.append(c)
 
     locs[1].wait()
+    locs[4].wait()
     w = a_v.shape[2]
     for bi in range(pattern.shape[0]):
         for bj in range(pattern.shape[1]):
-            wt = pattern[bi, bj].astype(F32)
+            wt = pat_s[bi, bj].astype(F32)
             rs = slice(bi * BLK, (bi + 1) * BLK)
             cs = slice(bj * BLK, (bj + 1) * BLK)
             r0, c0 = bi * BLK, bj * BLK
@@ -96,20 +98,44 @@
     lo = (half - hi.astype(F32)).astype(BF16)
     t = jnp.dot(um_v[...], jnp.concatenate([hi, lo], axis=1), preferred_element_type=F32)
     tbuf[...] = (t[:, :BLK] + t[:, BLK:]).reshape(tbuf.shape)
-    dx = remote(tbuf.at[:, 1 - x], x_in, x_send.at[0], x_recv.at[0], xp)
-    dx.start()
-    cxc = remote(cx.at[:, 1 - x], xc_in, x_send.at[1], x_recv.at[1], xp)
+    dx = []
+    for c in range(2):
+        dx.append(remote(tbuf.at[c, 1 - x], x_in.at[c], x_send.at[c], x_recv.at[c], xp))
+        dx[c].start()
+    cxc = remote(cx.at[:, 1 - x], xc_in, x_send.at[2], x_recv.at[2], xp)
     cxc.start()
-    sends += [dx, cxc]
-    dx.wait_recv()
-    sbuf[...] = tbuf[:, x] + x_in[...]
+    sends += dx + [cxc]
     zs = []
-    for d in range(1, n):
-        c = remote(sbuf.at[:, z_peer[d]], z_in.at[d], z_send.at[d], z_recv.at[d],
-                   (pole, z_peer[d], j))
-        c.start()
-        zs.append(c)
+    for c in range(2):
+        dx[c].wait_recv()
+        sbuf[c] = tbuf[c, x] + x_in[c]
+        for d in range(1, n):
+            s = c * n + d
+            zs.append(remote(sbuf.at[c, z_peer[d]], z_in.at[c, d], z_send.at[s],
+                             z_recv.at[s], (pole, z_peer[d], j)))
+            zs[-1].start()
     sends += zs
+
+    def piece(side, d, c, dev, send, recv):
+        slot = dall.at[h, side, z_from[d], c]
+        copy = remote(slot, slot, send, recv, dev)
+        copy.start()
+        sends.append(copy)
+        return copy
+
+    gz, gx, gc = [], {}, []
+    for c in range(2):
+        total = sbuf[c, me]
+        for d in range(1, n):
+            zs[c * (n - 1) + d - 1].wait_recv()
+            total = total + z_in[c, d]
+        dall[h, x, me, c] = total
+        for d in range(1, n):
+            s = c * n + d
+            gz.append(piece(x, 0, c, (pole, z_peer[d], j), gz_send.at[s], gz_recv.at[s]))
+        s = c * n
+        gx[s] = piece(x, 0, c, xp, gx_send.at[s], gx_recv.at[s])
+        gc.append(piece(x, 0, c, sib, gc_send.at[s], gc_recv.at[s]))
 
     cxc.wait_recv()
     call[h, x] = (cx[:, x] + xc_in[...]).astype(BF16)
@@ -119,42 +145,22 @@
     col_s.start()
     sends += [col_x, col_s]
 
-    total = sbuf[:, me]
-    for d in range(1, n):
-        zs[d - 1].wait_recv()
-        total = total + z_in[d]
-    dall[h, x, me] = total
-
-    def piece(side, d, dev, send, recv):
-        slot = dall.at[h, side, z_from[d]]
-        c = remote(slot, slot, send, recv, dev)
-        c.start()
-        sends.append(c)
-        return c
-
-    mine = dall.at[h, x, me]
-    gz = []
-    for d in range(1, n):
-        c = remote(mine, mine, gz_send.at[d], gz_recv.at[d], (pole, z_peer[d], j))
-        c.start()
-        sends.append(c)
-        gz.append(c)
-    gx = [piece(x, 0, xp, gx_send.at[0], gx_recv.at[0])]
-    gc = [piece(x, 0, sib, gc_send.at[0], gc_recv.at[0])]
-
+    for c in range(2):
+        for d in range(1, n):
+            s = c * n + d
+            gz[c * (n - 1) + d - 1].wait_recv()
+            gx[s] = piece(x, d, c, xp, gx_send.at[s], gx_recv.at[s])
+            gc.append(piece(x, d, c, sib, gc_send.at[s], gc_recv.at[s]))
     col_x.wait_recv()
     other = call.at[h, 1 - x]
     col_f = remote(other, other, c_send.at[2], c_recv.at[2], sib)
     col_f.start()
     sends.append(col_f)
-
-    for d in range(1, n):
-        gz[d - 1].wait_recv()
-        gx.append(piece(x, d, xp, gx_send.at[d], gx_recv.at[d]))
-        gc.append(piece(x, d, sib, gc_send.at[d], gc_recv.at[d]))
-    for d in range(n):
-        gx[d].wait_recv()
-        gc.append(piece(1 - x, d, sib, gc_send.at[n + d], gc_recv.at[n + d]))
+    for c in range(2):
+        for d in range(n):
+            s = c * n + d
+            gx[s].wait_recv()
+            gc.append(piece(1 - x, d, c, sib, gc_send.at[2 * n + s], gc_recv.at[2 * n + s]))
 
     col_s.wait_recv()
     col_f.wait_recv()
@@ -179,7 +185,7 @@
     w = ainv.shape[2]
     pr = BLK // n
     dma = pltpu.SemaphoreType.DMA
-    hbm = pl.BlockSpec(memory_space=pl.ANY)
+    hbm = pl.BlockSpec(memory_space=pltpu.HBM)
     vmem = pl.BlockSpec(memory_space=pltpu.VMEM)
     return pl.pallas_call(
         functools.partial(kernel, n),
@@ -187,9 +193,10 @@
             jax.ShapeDtypeStruct((2, w, w), BF16),
             jax.ShapeDtypeStruct((2, w, w), F32),
         ),
-        in_specs=[hbm, hbm, hbm, hbm, pl.BlockSpec(memory_space=pltpu.SMEM)],
+        in_specs=[hbm] * 5,
         out_specs=(vmem, vmem),
         scratch_shapes=[
+            pltpu.SMEM((2, 2), jnp.int32),
             pltpu.VMEM((2, w, w), BF16),
             pltpu.VMEM((2, w, w), BF16),
             pltpu.VMEM((2, w, w), F32),
@@ -203,24 +210,25 @@
             pltpu.VMEM((2, n, pr, BLK), F32),
             pltpu.VMEM((2, BLK, BLK), F32),
             pltpu.VMEM((2, n, pr, BLK), F32),
-            pltpu.VMEM((n, 2, pr, BLK), F32),
+            pltpu.VMEM((2, n, pr, BLK), F32),
             pltpu.VMEM((2, 2, n, 2, pr, BLK), F32),
             pltpu.VMEM((2, 2, 2, BLK, BLK), BF16),
-            dma((4,)),
+            dma((5,)),
             dma((n,)), dma((n,)),
             dma, dma,
-            dma((2,)), dma((2,)),
-            dma((n,)), dma((n,)),
-            dma((n,)), dma((n,)),
-            dma((n,)), dma((n,)),
+            dma((3,)), dma((3,)),
             dma((2 * n,)), dma((2 * n,)),
+            dma((2 * n,)), dma((2 * n,)),
+            dma((2 * n,)), dma((2 * n,)),
+            dma((4 * n,)), dma((4 * n,)),
             dma((3,)), dma((3,)),
         ],
         compiler_params=pltpu.CompilerParams(
             collective_id=0, has_side_effects=True, vmem_limit_bytes=48 * 2**20),
         cost_estimate=pl.CostEstimate(
             flops=12 * w**3, bytes_accessed=12 * w * w, transcendentals=0),
-    )(ainv, panel, upanel, dinv, pattern)
+    )(*(pltpu.with_memory_space_constraint(v, pltpu.HBM)
+        for v in (ainv, panel, upanel, dinv, pattern)))
 
 
 def complex_dot(left_re, left_im, right_re, right_im):

time: 38.7 us -> 32.1 us (0.83)
  local copies, waits for them, and re-layouts: 5.95 us -> 1.5 us
  Pallas kernels: 31.6 us -> 29.8 us
    unnamed x12 -> x2, local copies, waits for them, and re-layouts: 5.95 us -> 1.5 us
    pallas_call x1, Pallas kernels: 31.6 us -> 29.8 us  [fused(): pl.pallas_call(functools.partial(kernel, n), out_shape=(jax.ShapeDtypeStr...]
where the time goes in v2:
time: 32.1 us; the launch traced here: 31.9 us
  Pallas kernels  29.8 us (93%)
  local copies, waits for them, and re-layouts  1.5 us (5%)
  between operations  0.64 us (2%)
    pallas_call x1, Pallas kernels, fused(): pl.pallas_call(functools.partial(kernel, n), out_shape=(jax.ShapeDtypeStr...  29.8 us
    unnamed x2, local copies, waits for them, and re-layouts  1.5 us

profile of v2, /device:TPU:0, one launch (start us, length us, event | category | flops | bytes accessed | tf_op | source)
XLA Modules:
  0.0 31.9 jit_solution(4525876885334722164)
XLA Ops:
  0.6 29.8 %shard_map.68 = (bf16[2,256,256]{2,1,0:T(8,128)(2,1)S(1)}, f32[2,256,256]{2,1,0:T(8,128)S(1)}) custom-call(bf16[2,256,256]{2,1,0:T(8,128)(2,1)} %ainv.1, bf16[2,1,1,64,256]{4,3,2,1,0:T(8,128)(2,1)} %panel.1, bf16[2,256,256]{2,1,0:T(8,128)(2,1)} %upanel.1, f32[2,256,256]{2,1,0:T(8,128)} %dinv.1, s32[2,2]{1,0:T(2,128)} %pattern.1), custom_call_target="tpu_custom_call" | custom-call | flops 201326592 | bytes 786432 | tf_op jit(solution)/shard_map/pallas_call | solution.py:190
  30.4 0.7 %copy.9 = bf16[2,256,256]{2,1,0:T(8,128)(2,1)} copy(bf16[2,256,256]{2,1,0:T(8,128)(2,1)S(1)} %get-tuple-element.4) | data formatting | bytes 524288
  31.1 0.8 %copy.10 = f32[2,256,256]{2,1,0:T(8,128)} copy(f32[2,256,256]{2,1,0:T(8,128)S(1)} %get-tuple-element.5) | data formatting | bytes 1048576

commit v3 on v2

--- a/solution.py
+++ b/solution.py
@@ -14,8 +14,8 @@
 
 
 def kernel(n, ainv, panel, upanel, dinv, pattern, col_out, diag_out,
-           pat_s, a_v, u_v, d_v, low, m_v, um_v, part, core_in, cx, tbuf, x_in, xc_in,
-           sbuf, z_in, dall, call,
+           pat_s, a_v, u_v, d_v, low, m_v, um_v, part, core_in, cx, xc_in, call,
+           tbuf, d_in, s1, x_in, sbuf, z_in, dall,
            loc_sem, p_send, p_recv, b_send, b_recv, x_send, x_recv, z_send, z_recv,
            gz_send, gz_recv, gx_send, gx_recv, gc_send, gc_recv, c_send, c_recv):
     pole = lax.axis_index("pole")
@@ -28,6 +28,7 @@
     z_from = [lax.rem(me + n - d, n) for d in range(n)]
     sib = (pole, me, j + 1 - 2 * h)
     xp = (pole, me, lax.rem(j + 2, 4))
+    lanes = [slice(a * BLK, (a + 1) * BLK) for a in range(2)]
 
     def remote(src, dst, send, recv, device):
         return pltpu.make_async_remote_copy(
@@ -36,11 +37,14 @@
 
     my_rows = pl.ds(pl.multiple_of(me * rows, rows), rows)
     locs = [
-        pltpu.make_async_copy(panel.at[:, 0, 0], low.at[:, my_rows], loc_sem.at[0]),
+        pltpu.make_async_copy(
+            panel.at[:, 0, 0, :, lanes[0]], low.at[0, :, my_rows], loc_sem.at[0]),
         pltpu.make_async_copy(ainv, a_v, loc_sem.at[1]),
         pltpu.make_async_copy(upanel, u_v, loc_sem.at[2]),
         pltpu.make_async_copy(dinv, d_v, loc_sem.at[3]),
         pltpu.make_async_copy(pattern, pat_s, loc_sem.at[4]),
+        pltpu.make_async_copy(
+            panel.at[:, 0, 0, :, lanes[1]], low.at[1, :, my_rows], loc_sem.at[5]),
     ]
     for c in locs:
         c.start()
@@ -51,13 +55,15 @@
     pl.semaphore_wait(barrier, len(others))
 
     sends = []
-    gathers = []
-    for d in range(1, n):
-        c = remote(panel.at[:, 0, 0], low.at[:, my_rows], p_send.at[d], p_recv.at[d],
-                   (pole, z_peer[d], j))
-        c.start()
-        gathers.append(c)
-        sends.append(c)
+    gathers = [[], []]
+    for a in range(2):
+        for d in (2, 1, 3) if n == 4 else range(1, n):
+            k = a * n + d
+            c = remote(panel.at[:, 0, 0, :, lanes[a]], low.at[a, :, my_rows],
+                       p_send.at[k], p_recv.at[k], (pole, z_peer[d], j))
+            c.start()
+            gathers[a].append(c)
+            sends.append(c)
 
     locs[1].wait()
     locs[4].wait()
@@ -80,63 +86,77 @@
     um_v[w:, w:] = u_v[0]
     um_v[:w, w:] = -u_v[1]
     um_v[w:, :w] = u_v[1]
-    locs[0].wait()
-    for c in gathers:
-        c.wait_recv()
-
-    prod = jnp.dot(m_v[...], low[...].reshape(2 * w, w), preferred_element_type=F32)
-    part[0] = prod[:, :BLK]
-    part[1] = prod[:, BLK:]
-    c = remote(part.at[1 - h], core_in, b_send, b_recv, sib)
-    c.start()
-    c.wait_recv()
-    sends.append(c)
-
-    half = part[h] + core_in[...]
-    cx[...] = half.reshape(cx.shape)
-    hi = half.astype(BF16)
-    lo = (half - hi.astype(F32)).astype(BF16)
-    t = jnp.dot(um_v[...], jnp.concatenate([hi, lo], axis=1), preferred_element_type=F32)
-    tbuf[...] = (t[:, :BLK] + t[:, BLK:]).reshape(tbuf.shape)
-    dx = []
-    for c in range(2):
-        dx.append(remote(tbuf.at[c, 1 - x], x_in.at[c], x_send.at[c], x_recv.at[c], xp))
-        dx[c].start()
+
+    def product(a):
+        locs[(0, 5)[a]].wait()
+        for c in gathers[a]:
+            c.wait_recv()
+        p = jnp.dot(m_v[...], low[a].reshape(2 * w, BLK), preferred_element_type=F32)
+        part[a] = p
+        hi = p.astype(BF16)
+        lo = (p - hi.astype(F32)).astype(BF16)
+        t = jnp.dot(um_v[...], jnp.concatenate([hi, lo], axis=1), preferred_element_type=F32)
+        tbuf[a] = (t[:, :BLK] + t[:, BLK:]).reshape(tbuf.shape[1:])
+        c = remote(tbuf.at[a, :, 1 - h], d_in.at[a], b_send.at[a], b_recv.at[a], sib)
+        c.start()
+        return c
+
+    def over_core(a):
+        dc[a].wait_recv()
+        s1[a] = tbuf[a, :, h] + d_in[a]
+        c = remote(s1.at[a, :, 1 - x], x_in.at[a], x_send.at[a], x_recv.at[a], xp)
+        c.start()
+        return c
+
+    def over_x(a):
+        dx[a].wait_recv()
+        sbuf[a] = s1[a, :, x] + x_in[a]
+        zs = []
+        for d in range(1, n):
+            k = a * n + d
+            c = remote(sbuf.at[a, :, z_peer[d]], z_in.at[a, d], z_send.at[k],
+                       z_recv.at[k], (pole, z_peer[d], j))
+            c.start()
+            zs.append(c)
+        return zs
+
+    def piece(side, d, a, dev, send, recv):
+        slot = dall.at[h, side, z_from[d], a]
+        c = remote(slot, slot, send, recv, dev)
+        c.start()
+        sends.append(c)
+        return c
+
+    gz, gx, gc = {}, {}, []
+
+    def over_z(a):
+        total = sbuf[a, :, me]
+        for d in range(1, n):
+            zs[a][d - 1].wait_recv()
+            total = total + z_in[a, d]
+        dall[h, x, me, a] = total
+        for d in range(1, n):
+            k = a * n + d
+            gz[k] = piece(x, 0, a, (pole, z_peer[d], j), gz_send.at[k], gz_recv.at[k])
+        k = a * n
+        gx[k] = piece(x, 0, a, xp, gx_send.at[k], gx_recv.at[k])
+        gc.append(piece(x, 0, a, sib, gc_send.at[k], gc_recv.at[k]))
+
+    dc, dx, zs = [], [], []
+    dc.append(product(0))
+    dx.append(over_core(0))
+    dc.append(product(1))
+    cb = remote(part.at[1 - h], core_in, b_send.at[2], b_recv.at[2], sib)
+    cb.start()
+    zs.append(over_x(0))
+    dx.append(over_core(1))
+    cb.wait_recv()
+    cx[...] = (part[h] + core_in[...]).reshape(cx.shape)
     cxc = remote(cx.at[:, 1 - x], xc_in, x_send.at[2], x_recv.at[2], xp)
     cxc.start()
-    sends += dx + [cxc]
-    zs = []
-    for c in range(2):
-        dx[c].wait_recv()
-        sbuf[c] = tbuf[c, x] + x_in[c]
-        for d in range(1, n):
-            s = c * n + d
-            zs.append(remote(sbuf.at[c, z_peer[d]], z_in.at[c, d], z_send.at[s],
-                             z_recv.at[s], (pole, z_peer[d], j)))
-            zs[-1].start()
-    sends += zs
-
-    def piece(side, d, c, dev, send, recv):
-        slot = dall.at[h, side, z_from[d], c]
-        copy = remote(slot, slot, send, recv, dev)
-        copy.start()
-        sends.append(copy)
-        return copy
-
-    gz, gx, gc = [], {}, []
-    for c in range(2):
-        total = sbuf[c, me]
-        for d in range(1, n):
-            zs[c * (n - 1) + d - 1].wait_recv()
-            total = total + z_in[c, d]
-        dall[h, x, me, c] = total
-        for d in range(1, n):
-            s = c * n + d
-            gz.append(piece(x, 0, c, (pole, z_peer[d], j), gz_send.at[s], gz_recv.at[s]))
-        s = c * n
-        gx[s] = piece(x, 0, c, xp, gx_send.at[s], gx_recv.at[s])
-        gc.append(piece(x, 0, c, sib, gc_send.at[s], gc_recv.at[s]))
-
+    zs.append(over_x(1))
+    sends += dc + dx + zs[0] + zs[1] + [cb, cxc]
+    over_z(0)
     cxc.wait_recv()
     call[h, x] = (cx[:, x] + xc_in[...]).astype(BF16)
     col_x = remote(call.at[h, x], call.at[h, x], c_send.at[0], c_recv.at[0], xp)
@@ -144,46 +164,47 @@
     col_x.start()
     col_s.start()
     sends += [col_x, col_s]
-
-    for c in range(2):
+    over_z(1)
+    for a in range(2):
         for d in range(1, n):
-            s = c * n + d
-            gz[c * (n - 1) + d - 1].wait_recv()
-            gx[s] = piece(x, d, c, xp, gx_send.at[s], gx_recv.at[s])
-            gc.append(piece(x, d, c, sib, gc_send.at[s], gc_recv.at[s]))
-    col_x.wait_recv()
-    other = call.at[h, 1 - x]
-    col_f = remote(other, other, c_send.at[2], c_recv.at[2], sib)
-    col_f.start()
-    sends.append(col_f)
-    for c in range(2):
+            k = a * n + d
+            gz[k].wait_recv()
+            gx[k] = piece(x, d, a, xp, gx_send.at[k], gx_recv.at[k])
+            gc.append(piece(x, d, a, sib, gc_send.at[k], gc_recv.at[k]))
+        if a == 0:
+            col_x.wait_recv()
+            other = call.at[h, 1 - x]
+            col_f = remote(other, other, c_send.at[2], c_recv.at[2], sib)
+            col_f.start()
+            sends.append(col_f)
         for d in range(n):
-            s = c * n + d
-            gx[s].wait_recv()
-            gc.append(piece(1 - x, d, c, sib, gc_send.at[2 * n + s], gc_recv.at[2 * n + s]))
+            k = a * n + d
+            gx[k].wait_recv()
+            gc.append(piece(1 - x, d, a, sib, gc_send.at[2 * n + k], gc_recv.at[2 * n + k]))
 
     col_s.wait_recv()
     col_f.wait_recv()
     for a in range(2):
         for b in range(2):
-            col_out[:, b * BLK:(b + 1) * BLK, a * BLK:(a + 1) * BLK] = call[a, b]
+            col_out[:, b * BLK:(b + 1) * BLK, lanes[a]] = call[a, b]
     locs[3].wait()
     for c in gc:
         c.wait_recv()
-    pr = dall.shape[4]
-    for a in range(2):
+    pr = dall.shape[5]
+    for g in range(2):
         for b in range(2):
             for k in range(n):
-                rs = slice(b * BLK + k * pr, b * BLK + (k + 1) * pr)
-                cs = slice(a * BLK, (a + 1) * BLK)
-                diag_out[:, rs, cs] = d_v[:, rs, cs] - dall[a, b, k]
+                r0 = g * BLK + (b * n + k) * pr
+                for a in range(2):
+                    diag_out[:, r0:r0 + pr, lanes[a]] = (
+                        d_v[:, r0:r0 + pr, lanes[a]] - dall[g, b, k, a])
     for c in sends:
         c.wait_send()
 
 
 def fused(n, ainv, panel, upanel, dinv, pattern):
     w = ainv.shape[2]
-    pr = BLK // n
+    pr = BLK // 2 // n
     dma = pltpu.SemaphoreType.DMA
     hbm = pl.BlockSpec(memory_space=pltpu.HBM)
     vmem = pl.BlockSpec(memory_space=pltpu.VMEM)
@@ -200,22 +221,24 @@
             pltpu.VMEM((2, w, w), BF16),
             pltpu.VMEM((2, w, w), BF16),
             pltpu.VMEM((2, w, w), F32),
-            pltpu.VMEM((2, w, w), BF16),
+            pltpu.VMEM((2, 2, w, BLK), BF16),
             pltpu.VMEM((2 * w, 2 * w), BF16),
             pltpu.VMEM((2 * w, 2 * w), BF16),
             pltpu.VMEM((2, 2 * w, BLK), F32),
             pltpu.VMEM((2 * w, BLK), F32),
             pltpu.VMEM((2, 2, BLK, BLK), F32),
+            pltpu.VMEM((2, BLK, BLK), F32),
+            pltpu.VMEM((2, 2, 2, BLK, BLK), BF16),
+            pltpu.VMEM((2, 2, 2, 2, n, pr, BLK), F32),
+            pltpu.VMEM((2, 2, 2, n, pr, BLK), F32),
+            pltpu.VMEM((2, 2, 2, n, pr, BLK), F32),
             pltpu.VMEM((2, 2, n, pr, BLK), F32),
-            pltpu.VMEM((2, n, pr, BLK), F32),
-            pltpu.VMEM((2, BLK, BLK), F32),
-            pltpu.VMEM((2, n, pr, BLK), F32),
-            pltpu.VMEM((2, n, pr, BLK), F32),
-            pltpu.VMEM((2, 2, n, 2, pr, BLK), F32),
-            pltpu.VMEM((2, 2, 2, BLK, BLK), BF16),
-            dma((5,)),
-            dma((n,)), dma((n,)),
-            dma, dma,
+            pltpu.VMEM((2, 2, n, pr, BLK), F32),
+            pltpu.VMEM((2, n, 2, pr, BLK), F32),
+            pltpu.VMEM((2, 2, n, 2, 2, pr, BLK), F32),
+            dma((6,)),
+            dma((2 * n,)), dma((2 * n,)),
+            dma((3,)), dma((3,)),
             dma((3,)), dma((3,)),
             dma((2 * n,)), dma((2 * n,)),
             dma((2 * n,)), dma((2 * n,)),

time: 32.1 us -> 34.2 us (1.065)
  Pallas kernels: 29.8 us -> 31.9 us
    pallas_call x1, Pallas kernels: 29.8 us -> 31.9 us  [fused(): pl.pallas_call(functools.partial(kernel, n), out_shape=(jax.ShapeDtypeStr...]
where the time goes in v3:
time: 34.2 us; the launch traced here: 34.1 us
  Pallas kernels  31.9 us (93%)
  local copies, waits for them, and re-layouts  1.5 us (4%)
  between operations  0.64 us (2%)
    pallas_call x1, Pallas kernels, fused(): pl.pallas_call(functools.partial(kernel, n), out_shape=(jax.ShapeDtypeStr...  31.9 us
    unnamed x2, local copies, waits for them, and re-layouts  1.5 us

profile of v3, /device:TPU:0, one launch (start us, length us, event | category | flops | bytes accessed | tf_op | source)
XLA Modules:
  0.0 34.1 jit_solution(11838789145281692578)
XLA Ops:
  0.6 31.9 %shard_map.68 = (bf16[2,256,256]{2,1,0:T(8,128)(2,1)S(1)}, f32[2,256,256]{2,1,0:T(8,128)S(1)}) custom-call(bf16[2,256,256]{2,1,0:T(8,128)(2,1)} %ainv.1, bf16[2,1,1,64,256]{4,3,2,1,0:T(8,128)(2,1)} %panel.1, bf16[2,256,256]{2,1,0:T(8,128)(2,1)} %upanel.1, f32[2,256,256]{2,1,0:T(8,128)} %dinv.1, s32[2,2]{1,0:T(2,128)} %pattern.1), custom_call_target="tpu_custom_call" | custom-call | flops 201326592 | bytes 786432 | tf_op jit(solution)/shard_map/pallas_call | solution.py:211
  32.6 0.7 %copy.9 = bf16[2,256,256]{2,1,0:T(8,128)(2,1)} copy(bf16[2,256,256]{2,1,0:T(8,128)(2,1)S(1)} %get-tuple-element.4) | data formatting | bytes 524288
  33.3 0.8 %copy.10 = f32[2,256,256]{2,1,0:T(8,128)} copy(f32[2,256,256]{2,1,0:T(8,128)S(1)} %get-tuple-element.5) | data formatting | bytes 1048576

commit v4 on v2

--- a/solution.py
+++ b/solution.py
@@ -14,10 +14,10 @@
 
 
 def kernel(n, ainv, panel, upanel, dinv, pattern, col_out, diag_out,
-           pat_s, a_v, u_v, d_v, low, m_v, um_v, part, core_in, cx, tbuf, x_in, xc_in,
-           sbuf, z_in, dall, call,
-           loc_sem, p_send, p_recv, b_send, b_recv, x_send, x_recv, z_send, z_recv,
-           gz_send, gz_recv, gx_send, gx_recv, gc_send, gc_recv, c_send, c_recv):
+           pat_s, a_v, u_v, d_v, low, m_v, um_v, part, core_in, cx, tbuf, xc_in,
+           r_in, dall, call,
+           loc_sem, p_send, p_recv, b_send, b_recv, x_send, x_recv, r_send, r_recv,
+           g_send, g_recv, gc_send, gc_recv, c_send, c_recv):
     pole = lax.axis_index("pole")
     me = lax.axis_index("prow")
     j = lax.axis_index("pcol")
@@ -28,6 +28,9 @@
     z_from = [lax.rem(me + n - d, n) for d in range(n)]
     sib = (pole, me, j + 1 - 2 * h)
     xp = (pole, me, lax.rem(j + 2, 4))
+    hops = [(f, d) for d in (2, 3, 1, 0) for f in (1, 0) if (f, d) != (0, 0)]
+    spot = [(lax.rem(x + f, 2), z_peer[d]) for f, d in hops]
+    seven = [(pole, zz, 2 * xx + h) for xx, zz in spot]
 
     def remote(src, dst, send, recv, device):
         return pltpu.make_async_remote_copy(
@@ -45,7 +48,7 @@
     for c in locs:
         c.start()
     barrier = pltpu.get_barrier_semaphore()
-    others = [(pole, z_peer[d], j) for d in range(1, n)] + [sib, xp]
+    others = seven + [sib]
     for dev in others:
         pl.semaphore_signal(barrier, inc=1, device_id=dev, device_id_type=MESH)
     pl.semaphore_wait(barrier, len(others))
@@ -98,44 +101,31 @@
     lo = (half - hi.astype(F32)).astype(BF16)
     t = jnp.dot(um_v[...], jnp.concatenate([hi, lo], axis=1), preferred_element_type=F32)
     tbuf[...] = (t[:, :BLK] + t[:, BLK:]).reshape(tbuf.shape)
-    dx = []
-    for c in range(2):
-        dx.append(remote(tbuf.at[c, 1 - x], x_in.at[c], x_send.at[c], x_recv.at[c], xp))
-        dx[c].start()
-    cxc = remote(cx.at[:, 1 - x], xc_in, x_send.at[2], x_recv.at[2], xp)
+    k7 = len(hops)
+    rs = []
+    for c in range(2):
+        for i, (xx, zz) in enumerate(spot):
+            s = c * k7 + i
+            rs.append(remote(tbuf.at[c, xx, zz], r_in.at[s], r_send.at[s], r_recv.at[s],
+                             seven[i]))
+            rs[s].start()
+    cxc = remote(cx.at[:, 1 - x], xc_in, x_send, x_recv, xp)
     cxc.start()
-    sends += dx + [cxc]
-    zs = []
-    for c in range(2):
-        dx[c].wait_recv()
-        sbuf[c] = tbuf[c, x] + x_in[c]
-        for d in range(1, n):
-            s = c * n + d
-            zs.append(remote(sbuf.at[c, z_peer[d]], z_in.at[c, d], z_send.at[s],
-                             z_recv.at[s], (pole, z_peer[d], j)))
-            zs[-1].start()
-    sends += zs
-
-    def piece(side, d, c, dev, send, recv):
-        slot = dall.at[h, side, z_from[d], c]
-        copy = remote(slot, slot, send, recv, dev)
-        copy.start()
-        sends.append(copy)
-        return copy
-
-    gz, gx, gc = [], {}, []
-    for c in range(2):
-        total = sbuf[c, me]
-        for d in range(1, n):
-            zs[c * (n - 1) + d - 1].wait_recv()
-            total = total + z_in[c, d]
-        dall[h, x, me, c] = total
-        for d in range(1, n):
-            s = c * n + d
-            gz.append(piece(x, 0, c, (pole, z_peer[d], j), gz_send.at[s], gz_recv.at[s]))
-        s = c * n
-        gx[s] = piece(x, 0, c, xp, gx_send.at[s], gx_recv.at[s])
-        gc.append(piece(x, 0, c, sib, gc_send.at[s], gc_recv.at[s]))
+    sends += rs + [cxc]
+
+    ag = []
+    for c in range(2):
+        total = tbuf[c, x, me]
+        for i in range(k7):
+            rs[c * k7 + i].wait_recv()
+            total = total + r_in[c * k7 + i]
+        dall[h, c, x, me] = total
+        mine = dall.at[h, c, x, me]
+        for i in range(k7):
+            s = c * k7 + i
+            ag.append(remote(mine, mine, g_send.at[s], g_recv.at[s], seven[i]))
+            ag[s].start()
+    sends += ag
 
     cxc.wait_recv()
     call[h, x] = (cx[:, x] + xc_in[...]).astype(BF16)
@@ -144,23 +134,19 @@
     col_x.start()
     col_s.start()
     sends += [col_x, col_s]
-
-    for c in range(2):
-        for d in range(1, n):
-            s = c * n + d
-            gz[c * (n - 1) + d - 1].wait_recv()
-            gx[s] = piece(x, d, c, xp, gx_send.at[s], gx_recv.at[s])
-            gc.append(piece(x, d, c, sib, gc_send.at[s], gc_recv.at[s]))
     col_x.wait_recv()
     other = call.at[h, 1 - x]
     col_f = remote(other, other, c_send.at[2], c_recv.at[2], sib)
     col_f.start()
     sends.append(col_f)
-    for c in range(2):
-        for d in range(n):
-            s = c * n + d
-            gx[s].wait_recv()
-            gc.append(piece(1 - x, d, c, sib, gc_send.at[2 * n + s], gc_recv.at[2 * n + s]))
+
+    gc = []
+    for c in range(2):
+        for i in range(k7):
+            ag[c * k7 + i].wait_recv()
+        gc.append(remote(dall.at[h, c], dall.at[h, c], gc_send.at[c], gc_recv.at[c], sib))
+        gc[c].start()
+    sends += gc
 
     col_s.wait_recv()
     col_f.wait_recv()
@@ -168,15 +154,14 @@
         for b in range(2):
             col_out[:, b * BLK:(b + 1) * BLK, a * BLK:(a + 1) * BLK] = call[a, b]
     locs[3].wait()
-    for c in gc:
-        c.wait_recv()
     pr = dall.shape[4]
-    for a in range(2):
-        for b in range(2):
-            for k in range(n):
-                rs = slice(b * BLK + k * pr, b * BLK + (k + 1) * pr)
+    for c in range(2):
+        gc[c].wait_recv()
+        for a in range(2):
+            for b in range(2):
+                rs = slice(b * BLK, (b + 1) * BLK)
                 cs = slice(a * BLK, (a + 1) * BLK)
-                diag_out[:, rs, cs] = d_v[:, rs, cs] - dall[a, b, k]
+                diag_out[c, rs, cs] = d_v[c, rs, cs] - dall[a, c, b].reshape(n * pr, BLK)
     for c in sends:
         c.wait_send()
 
@@ -207,20 +192,17 @@
             pltpu.VMEM((2 * w, BLK), F32),
             pltpu.VMEM((2, 2, BLK, BLK), F32),
             pltpu.VMEM((2, 2, n, pr, BLK), F32),
-            pltpu.VMEM((2, n, pr, BLK), F32),
             pltpu.VMEM((2, BLK, BLK), F32),
-            pltpu.VMEM((2, n, pr, BLK), F32),
-            pltpu.VMEM((2, n, pr, BLK), F32),
-            pltpu.VMEM((2, 2, n, 2, pr, BLK), F32),
+            pltpu.VMEM((4 * n - 2, pr, BLK), F32),
+            pltpu.VMEM((2, 2, 2, n, pr, BLK), F32),
             pltpu.VMEM((2, 2, 2, BLK, BLK), BF16),
             dma((5,)),
             dma((n,)), dma((n,)),
             dma, dma,
-            dma((3,)), dma((3,)),
-            dma((2 * n,)), dma((2 * n,)),
-            dma((2 * n,)), dma((2 * n,)),
-            dma((2 * n,)), dma((2 * n,)),
-            dma((4 * n,)), dma((4 * n,)),
+            dma, dma,
+            dma((4 * n - 2,)), dma((4 * n - 2,)),
+            dma((4 * n - 2,)), dma((4 * n - 2,)),
+            dma((2,)), dma((2,)),
             dma((3,)), dma((3,)),
         ],
         compiler_params=pltpu.CompilerParams(

time: 32.1 us -> 31.5 us (0.981)
  Pallas kernels: 29.8 us -> 29.2 us
    pallas_call x1, Pallas kernels: 29.8 us -> 29.2 us  [fused(): pl.pallas_call(functools.partial(kernel, n), out_shape=(jax.ShapeDtypeStr...]
where the time goes in v4:
time: 31.5 us; the launch traced here: 31.3 us
  Pallas kernels  29.2 us (93%)
  local copies, waits for them, and re-layouts  1.5 us (5%)
  between operations  0.64 us (2%)
    pallas_call x1, Pallas kernels, fused(): pl.pallas_call(functools.partial(kernel, n), out_shape=(jax.ShapeDtypeStr...  29.2 us
    unnamed x2, local copies, waits for them, and re-layouts  1.5 us

profile of v4, /device:TPU:0, one launch (start us, length us, event | category | flops | bytes accessed | tf_op | source)
XLA Modules:
  0.0 31.3 jit_solution(1210163559761595599)
XLA Ops:
  0.6 29.2 %shard_map.68 = (bf16[2,256,256]{2,1,0:T(8,128)(2,1)S(1)}, f32[2,256,256]{2,1,0:T(8,128)S(1)}) custom-call(bf16[2,256,256]{2,1,0:T(8,128)(2,1)} %ainv.1, bf16[2,1,1,64,256]{4,3,2,1,0:T(8,128)(2,1)} %panel.1, bf16[2,256,256]{2,1,0:T(8,128)(2,1)} %upanel.1, f32[2,256,256]{2,1,0:T(8,128)} %dinv.1, s32[2,2]{1,0:T(2,128)} %pattern.1), custom_call_target="tpu_custom_call" | custom-call | flops 201326592 | bytes 786432 | tf_op jit(solution)/shard_map/pallas_call | solution.py:175
  29.8 0.7 %copy.9 = bf16[2,256,256]{2,1,0:T(8,128)(2,1)} copy(bf16[2,256,256]{2,1,0:T(8,128)(2,1)S(1)} %get-tuple-element.4) | data formatting | bytes 524288
  30.5 0.8 %copy.10 = f32[2,256,256]{2,1,0:T(8,128)} copy(f32[2,256,256]{2,1,0:T(8,128)S(1)} %get-tuple-element.5) | data formatting | bytes 1048576

commit v5 on v4

--- a/solution.py
+++ b/solution.py
@@ -55,7 +55,7 @@
 
     sends = []
     gathers = []
-    for d in range(1, n):
+    for d in (2, 1, 3):
         c = remote(panel.at[:, 0, 0], low.at[:, my_rows], p_send.at[d], p_recv.at[d],
                    (pole, z_peer[d], j))
         c.start()
@@ -87,13 +87,18 @@
     for c in gathers:
         c.wait_recv()
 
-    prod = jnp.dot(m_v[...], low[...].reshape(2 * w, w), preferred_element_type=F32)
-    part[0] = prod[:, :BLK]
-    part[1] = prod[:, BLK:]
-    c = remote(part.at[1 - h], core_in, b_send, b_recv, sib)
-    c.start()
-    c.wait_recv()
-    sends.append(c)
+    full = low[...].reshape(2 * w, w)
+    swap = []
+    for c in range(2):
+        rs = slice(c * w, (c + 1) * w)
+        prod = jnp.dot(m_v[rs, :], full, preferred_element_type=F32)
+        part[0, rs] = prod[:, :BLK]
+        part[1, rs] = prod[:, BLK:]
+        swap.append(remote(part.at[1 - h, rs], core_in.at[rs], b_send.at[c], b_recv.at[c], sib))
+        swap[c].start()
+    for c in swap:
+        c.wait_recv()
+    sends += swap
 
     half = part[h] + core_in[...]
     cx[...] = half.reshape(cx.shape)
@@ -198,7 +203,7 @@
             pltpu.VMEM((2, 2, 2, BLK, BLK), BF16),
             dma((5,)),
             dma((n,)), dma((n,)),
-            dma, dma,
+            dma((2,)), dma((2,)),
             dma, dma,
             dma((4 * n - 2,)), dma((4 * n - 2,)),
             dma((4 * n - 2,)), dma((4 * n - 2,)),

time: 31.5 us -> 31.4 us (level)
  no operation moved by 1% of the time
where the time goes in v5:
time: 31.4 us; the launch traced here: 31.2 us
  Pallas kernels  29.1 us (93%)
  local copies, waits for them, and re-layouts  1.5 us (5%)
  between operations  0.64 us (2%)
    pallas_call x1, Pallas kernels, fused(): pl.pallas_call(functools.partial(kernel, n), out_shape=(jax.ShapeDtypeStr...  29.1 us
    unnamed x2, local copies, waits for them, and re-layouts  1.5 us

profile of v5, /device:TPU:0, one launch (start us, length us, event | category | flops | bytes accessed | tf_op | source)
XLA Modules:
  0.0 31.2 jit_solution(8600580346687437470)
XLA Ops:
  0.6 29.1 %shard_map.68 = (bf16[2,256,256]{2,1,0:T(8,128)(2,1)S(1)}, f32[2,256,256]{2,1,0:T(8,128)S(1)}) custom-call(bf16[2,256,256]{2,1,0:T(8,128)(2,1)} %ainv.1, bf16[2,1,1,64,256]{4,3,2,1,0:T(8,128)(2,1)} %panel.1, bf16[2,256,256]{2,1,0:T(8,128)(2,1)} %upanel.1, f32[2,256,256]{2,1,0:T(8,128)} %dinv.1, s32[2,2]{1,0:T(2,128)} %pattern.1), custom_call_target="tpu_custom_call" | custom-call | flops 201326592 | bytes 786432 | tf_op jit(solution)/shard_map/pallas_call | solution.py:180
  29.7 0.7 %copy.9 = bf16[2,256,256]{2,1,0:T(8,128)(2,1)} copy(bf16[2,256,256]{2,1,0:T(8,128)(2,1)S(1)} %get-tuple-element.4) | data formatting | bytes 524288
  30.4 0.8 %copy.10 = f32[2,256,256]{2,1,0:T(8,128)} copy(f32[2,256,256]{2,1,0:T(8,128)S(1)} %get-tuple-element.5) | data formatting | bytes 1048576

commit v6 on v5

--- a/solution.py
+++ b/solution.py
@@ -28,7 +28,7 @@
     z_from = [lax.rem(me + n - d, n) for d in range(n)]
     sib = (pole, me, j + 1 - 2 * h)
     xp = (pole, me, lax.rem(j + 2, 4))
-    hops = [(f, d) for d in (2, 3, 1, 0) for f in (1, 0) if (f, d) != (0, 0)]
+    hops = [(f, d) for f in (1, 0) for d in (2, 1, 3, 0) if (f, d) != (0, 0)]
     spot = [(lax.rem(x + f, 2), z_peer[d]) for f, d in hops]
     seven = [(pole, zz, 2 * xx + h) for xx, zz in spot]
 

time: 31.4 us -> 31.8 us (1.013)
  Pallas kernels: 29.1 us -> 29.5 us
    pallas_call x1, Pallas kernels: 29.1 us -> 29.5 us  [fused(): pl.pallas_call(functools.partial(kernel, n), out_shape=(jax.ShapeDtypeStr...]
where the time goes in v6:
time: 31.8 us; the launch traced here: 31.6 us
  Pallas kernels  29.5 us (93%)
  local copies, waits for them, and re-layouts  1.5 us (5%)
  between operations  0.64 us (2%)
    pallas_call x1, Pallas kernels, fused(): pl.pallas_call(functools.partial(kernel, n), out_shape=(jax.ShapeDtypeStr...  29.5 us
    unnamed x2, local copies, waits for them, and re-layouts  1.5 us

profile of v6, /device:TPU:0, one launch (start us, length us, event | category | flops | bytes accessed | tf_op | source)
XLA Modules:
  0.0 31.6 jit_solution(8791850049571455114)
XLA Ops:
  0.6 29.5 %shard_map.68 = (bf16[2,256,256]{2,1,0:T(8,128)(2,1)S(1)}, f32[2,256,256]{2,1,0:T(8,128)S(1)}) custom-call(bf16[2,256,256]{2,1,0:T(8,128)(2,1)} %ainv.1, bf16[2,1,1,64,256]{4,3,2,1,0:T(8,128)(2,1)} %panel.1, bf16[2,256,256]{2,1,0:T(8,128)(2,1)} %upanel.1, f32[2,256,256]{2,1,0:T(8,128)} %dinv.1, s32[2,2]{1,0:T(2,128)} %pattern.1), custom_call_target="tpu_custom_call" | custom-call | flops 201326592 | bytes 786432 | tf_op jit(solution)/shard_map/pallas_call | solution.py:180
  30.1 0.7 %copy.9 = bf16[2,256,256]{2,1,0:T(8,128)(2,1)} copy(bf16[2,256,256]{2,1,0:T(8,128)(2,1)S(1)} %get-tuple-element.4) | data formatting | bytes 524288
  30.8 0.8 %copy.10 = f32[2,256,256]{2,1,0:T(8,128)} copy(f32[2,256,256]{2,1,0:T(8,128)S(1)} %get-tuple-element.5) | data formatting | bytes 1048576
